TPU v7x, 32 devices: a whole 2x2x4 slice. The times are simulated.
32 devices in a mesh: tm: 2 (over x), space: 16 (over z, y, core).
Axes of the slice: x: 2, y: 2, z: 4, core: 2. Of those that a mesh axis runs over, the one named last changes fastest.
Arguments:
- states: float32 [2, 3, 32, 128, 128], P('tm', None, 'space'), may hold values from -2 to 2
- viscosity: float32 [32, 128, 128], P('space'), may hold values from 0.2 to 0.6
Outputs:
- corrected: float32 [2, 3, 32, 128, 128], P('tm', None, 'space')
All inputs are finite; a program needn't handle non-finite values.
Results may differ from a plain program's by a relative error of at most 0.00002.
Values sent between devices are 32-bit elements; how exact they have to be, the bound alone decides.
A program may use at most 64 MiB of HBM per device.

v0:
```python
import jax
import jax.numpy as jnp
from jax import lax
from jax.sharding import PartitionSpec as P

FINE_STEP = 0.12
COARSE_STEP = 0.24


def padded_2(cells, sides, width):
    for axis, dim in sides:
        count = lax.axis_size(axis)
        head = lax.slice_in_dim(cells, 0, width, axis=dim)
        tail = lax.slice_in_dim(cells, cells.shape[dim] - width, cells.shape[dim], axis=dim)
        cells = jnp.concatenate(
            [
                lax.ppermute(tail, axis, [(i, (i + 1) % count) for i in range(count)]),
                cells,
                lax.ppermute(head, axis, [((i + 1) % count, i) for i in range(count)]),
            ],
            axis=dim,
        )
    return cells


def from_behind(value, axis, steps):
    count = lax.axis_size(axis)
    first, last = (max(0, -steps), min(count, count - steps))
    return lax.ppermute(value, axis, [(source, source + steps) for source in range(first, last)])


def advance_with(center, above, below, y_plus, y_minus, visc, step):
    x_plus = jnp.roll(center, -1, axis=-1)
    x_minus = jnp.roll(center, 1, axis=-1)
    laplace = above + below + (y_plus + y_minus) + (x_plus + x_minus) - 6.0 * center
    carried = (
        center[0:1] * (above - below) * 0.5
        + center[1:2] * (y_plus - y_minus) * 0.5
        + center[2:3] * (x_plus - x_minus) * 0.5
    )
    return center + step * (visc[None] * laplace - carried)


def advance(center, above, below, visc, step):
    y_plus = jnp.roll(center, -1, axis=-2)
    y_minus = jnp.roll(center, 1, axis=-2)
    return advance_with(center, above, below, y_plus, y_minus, visc, step)


def padded_step(padded, visc, step):
    return advance(padded[:, 1:-1], padded[:, 2:], padded[:, :-2], visc, step)


def coarse_update(field, visc, jump):
    padded = padded_2(field, (("space", 1),), 1)
    return padded_step(padded, visc, COARSE_STEP) + jump


def local(states, viscosity):
    own = states[0]
    padded = padded_2(own, (("space", 1),), 1)
    coarse_own = padded_step(padded, viscosity, COARSE_STEP)
    first = padded_step(padded, viscosity, FINE_STEP)
    padded_again = padded_2(first, (("space", 1),), 1)
    fine = padded_step(padded_again, viscosity, FINE_STEP)
    jump = fine - coarse_own
    groups = lax.axis_size("tm")
    position = lax.axis_index("tm")
    start = own
    for turn in range(groups):
        updated = coarse_update(start, viscosity, jump)
        if turn + 1 < groups:
            arrived = from_behind(updated, "tm", 1)
            start = jnp.where(
                position == turn, updated, jnp.where(position == turn + 1, arrived, start)
            )
        else:
            start = jnp.where(position == turn, updated, start)
    return start[None]


def solution(mesh):
    return jax.shard_map(
        local,
        mesh=mesh,
        in_specs=(P("tm", None, "space", None, None), P("space", None, None)),
        out_specs=P("tm", None, "space", None, None),
        check_vma=False,
    )
```

profile of v0, /device:TPU:0, one launch (start us, length us, event | category | flops | bytes accessed | tf_op | source)
XLA Modules:
  0.0 43.5 jit_solution(12082100245459656368)
XLA Ops:
  0.0 0.0 copy-start
  0.0 1.1 %fusion.11 = (f32[3,1,128,128]{3,2,1,0:T(8,128)S(1)}, f32[3,1,128,128]{3,2,1,0:T(8,128)S(1)}) fusion(f32[3,2,128,128]{3,2,1,0:T(8,128)} %bitcast.26), kind=kLoop, calls=%fused_computation.44 | loop fusion | bytes 786432 | tf_op jit(solution)/shard_map/slice | solution.py:13
  1.1 5.5 %collective-permute-start = (f32[3,1,128,128]{3,2,1,0:T(8,128)S(1)}, f32[3,1,128,128]{3,2,1,0:T(8,128)S(1)}, u32[]{:S(2)}, u32[]{:S(2)}) collective-permute-start(f32[3,1,128,128]{3,2,1,0:T(8,128)S(1)} %get-tuple-element.35), channel_id=1, source_target_pairs={{1,0},{2,1},{3,2},{4,3},{5,4},{6,5},{7,6},{8,7},{9,8},{10,9},{11,1... | collective-permute-start | bytes 589832 | tf_op jit(solution)/shard_map/ppermute | solution.py:19
  6.6 0.0 collective-permute-start.1
  6.6 0.0 copy-done
  6.6 0.1 fusion.12
  6.7 0.2 fusion.14
  6.8 0.2 fusion.15
  7.0 0.0 copy-start.1
  7.1 2.7 %collective-permute-done = f32[3,1,128,128]{3,2,1,0:T(8,128)S(1)} collective-permute-done((f32[3,1,128,128]{3,2,1,0:T(8,128)S(1)}, f32[3,1,128,128]{3,2,1,0:T(8,128)S(1)}, u32[]{:S(2)}, u32[]{:S(2)}) %collective-permute-start) | collective-permute-done | bytes 196640 | tf_op jit(solution)/shard_map/ppermute | solution.py:19
  9.8 4.6 %collective-permute-done.1 = f32[3,1,128,128]{3,2,1,0:T(8,128)S(1)} collective-permute-done((f32[3,1,128,128]{3,2,1,0:T(8,128)S(1)}, f32[3,1,128,128]{3,2,1,0:T(8,128)S(1)}, u32[]{:S(2)}, u32[]{:S(2)}) %collective-permute-start.1) | collective-permute-done | bytes 196640 | tf_op jit(solution)/shard_map/ppermute | solution.py:17
  14.4 0.0 copy-done.1
  14.4 0.5 %multiply_add_fusion = (f32[3,2,128,128]{3,2,1,0:T(8,128)S(1)}, f32[3,2,128,128]{3,2,1,0:T(8,128)S(1)}) fusion(f32[1,3,2,128,128]{4,3,2,1,0:T(8,128)S(1)} %copy-done, f32[2,128,128]{2,1,0:T(8,128)S(1)} %get-tuple-element.46, f32[2,128,128]{2,1,0:T(8,128)S(1)} %get-tuple-element.47, f32[2,128,128]{2,1,0:T(8,128)S(1)} %get-tuple-element.45, ...), kind=kLoop, calls=%fused_computation.21 | loop fusion | flops 2555904 | bytes 4063232 | tf_op jit(solution)/shard_map/add | solution.py:41
  14.9 0.1 fusion.7
  15.0 0.2 fusion.9
  15.2 0.2 fusion.10
  15.4 0.1 collective-permute-start.2
  15.5 0.5 %collective-permute-start.3 = (f32[3,1,128,128]{3,2,1,0:T(8,128)S(1)}, f32[3,1,128,128]{3,2,1,0:T(8,128)S(1)}, u32[]{:S(2)}, u32[]{:S(2)}) collective-permute-start(f32[3,1,128,128]{3,2,1,0:T(8,128)S(1)} %get-tuple-element.23), channel_id=1, source_target_pairs={{0,1},{1,2},{2,3},{3,4},{4,5},{5,6},{6,7},{7,8},{8,9},{9,10},{10,1... | collective-permute-start | bytes 589832 | tf_op jit(solution)/shard_map/ppermute | solution.py:17
  16.0 2.7 %collective-permute-done.2 = f32[3,1,128,128]{3,2,1,0:T(8,128)S(1)} collective-permute-done((f32[3,1,128,128]{3,2,1,0:T(8,128)S(1)}, f32[3,1,128,128]{3,2,1,0:T(8,128)S(1)}, u32[]{:S(2)}, u32[]{:S(2)}) %collective-permute-start.2) | collective-permute-done | bytes 196640 | tf_op jit(solution)/shard_map/ppermute | solution.py:19
  18.6 4.7 %collective-permute-done.3 = f32[3,1,128,128]{3,2,1,0:T(8,128)S(1)} collective-permute-done((f32[3,1,128,128]{3,2,1,0:T(8,128)S(1)}, f32[3,1,128,128]{3,2,1,0:T(8,128)S(1)}, u32[]{:S(2)}, u32[]{:S(2)}) %collective-permute-start.3) | collective-permute-done | bytes 196640 | tf_op jit(solution)/shard_map/ppermute | solution.py:17
  23.3 0.5 %fusion = (f32[3,2,128,128]{3,2,1,0:T(8,128)S(1)}, f32[3,2,128,128]{3,2,1,0:T(8,128)S(1)}) fusion(f32[3,2,128,128]{3,2,1,0:T(8,128)S(1)} %get-tuple-element.8, f32[1,3,2,128,128]{4,3,2,1,0:T(8,128)S(1)} %copy-done, f32[3,2,128,128]{3,2,1,0:T(8,128)S(1)} %get-tuple-element.7, f32[2,128,128]{2,1,0:T(8,128)S(1)} %get-tuple-element.33, ...), kind=kLoop, calls=%fused_computation.24 | loop fusion | flops 2949120 | bytes 4456448 | tf_op jit(solution)/shard_map/add | solution.py:56
  23.9 3.4 %collective-permute-start.4 = (f32[3,2,128,128]{3,2,1,0:T(8,128)S(1)}, f32[3,2,128,128]{3,2,1,0:T(8,128)S(1)}, u32[]{:S(2)}, u32[]{:S(2)}) collective-permute-start(f32[3,2,128,128]{3,2,1,0:T(8,128)S(1)} %get-tuple-element.5), channel_id=1, source_target_pairs={{0,16},{1,17},{2,18},{3,19},{4,20},{5,21},{6,22},{7,23},{8,24},{9,... | collective-permute-start | bytes 1179656 | tf_op jit(solution)/shard_map/ppermute | solution.py:29
  27.3 5.2 %collective-permute-done.4 = f32[3,2,128,128]{3,2,1,0:T(8,128)S(1)} collective-permute-done((f32[3,2,128,128]{3,2,1,0:T(8,128)S(1)}, f32[3,2,128,128]{3,2,1,0:T(8,128)S(1)}, u32[]{:S(2)}, u32[]{:S(2)}) %collective-permute-start.4) | collective-permute-done | bytes 393248 | tf_op jit(solution)/shard_map/ppermute | solution.py:29
  32.5 0.1 select_select_fusion
  32.6 0.1 fusion.2
  32.7 0.2 fusion.4
  32.8 0.2 fusion.5
  33.1 1.4 %collective-permute-start.5 = (f32[3,1,128,128]{3,2,1,0:T(8,128)S(1)}, f32[3,1,128,128]{3,2,1,0:T(8,128)S(1)}, u32[]{:S(2)}, u32[]{:S(2)}) collective-permute-start(f32[3,1,128,128]{3,2,1,0:T(8,128)S(1)} %get-tuple-element.13), channel_id=1, source_target_pairs={{1,0},{2,1},{3,2},{4,3},{5,4},{6,5},{7,6},{8,7},{9,8},{10,9},{11,1... | collective-permute-start | bytes 589832 | tf_op jit(solution)/shard_map/ppermute | solution.py:19
  34.5 0.0 collective-permute-start.6
  34.5 3.2 %collective-permute-done.5 = f32[3,1,128,128]{3,2,1,0:T(8,128)S(1)} collective-permute-done((f32[3,1,128,128]{3,2,1,0:T(8,128)S(1)}, f32[3,1,128,128]{3,2,1,0:T(8,128)S(1)}, u32[]{:S(2)}, u32[]{:S(2)}) %collective-permute-start.5) | collective-permute-done | bytes 196640 | tf_op jit(solution)/shard_map/ppermute | solution.py:19
  37.7 4.6 %collective-permute-done.6 = f32[3,1,128,128]{3,2,1,0:T(8,128)S(1)} collective-permute-done((f32[3,1,128,128]{3,2,1,0:T(8,128)S(1)}, f32[3,1,128,128]{3,2,1,0:T(8,128)S(1)}, u32[]{:S(2)}, u32[]{:S(2)}) %collective-permute-start.6) | collective-permute-done | bytes 196640 | tf_op jit(solution)/shard_map/ppermute | solution.py:17
  42.3 1.2 %select_bitcast_fusion = f32[1,3,2,128,128]{4,3,2,1,0:T(8,128)} fusion(f32[3,2,128,128]{3,2,1,0:T(8,128)S(1)} %select_select_fusion, f32[3,2,128,128]{3,2,1,0:T(8,128)S(1)} %get-tuple-element.6, f32[3,2,128,127]{3,2,1,0:T(8,128)S(1)} %get-tuple-element.19, f32[3,2,128,1]{3,2,1,0:T(8,128)S(1)} %get-tuple-element.21, ...), kind=kLoop, calls=%fused_computation.18 | loop fusion | flops 2752512 | bytes 3670017 | tf_op jit(solution)/shard_map/broadcast_in_dim | solution.py:79
  (8 shorter events, 0.2 us)
Async XLA Ops:
  0.0 6.6 %copy-start = (f32[1,3,2,128,128]{4,3,2,1,0:T(8,128)S(1)}, f32[1,3,2,128,128]{4,3,2,1,0:T(8,128)}, u32[]{:S(2)}) copy-start(f32[1,3,2,128,128]{4,3,2,1,0:T(8,128)} %param.2) | copy-start | bytes 1179652
  1.1 8.7 %collective-permute-start = (f32[3,1,128,128]{3,2,1,0:T(8,128)S(1)}, f32[3,1,128,128]{3,2,1,0:T(8,128)S(1)}, u32[]{:S(2)}, u32[]{:S(2)}) collective-permute-start(f32[3,1,128,128]{3,2,1,0:T(8,128)S(1)} %get-tuple-element.35), channel_id=1, source_target_pairs={{1,0},{2,1},{3,2},{4,3},{5,4},{6,5},{7,6},{8,7},{9,8},{10,9},{11,1... | collective-permute-start | bytes 589832 | tf_op jit(solution)/shard_map/ppermute | solution.py:19
  6.6 7.8 %collective-permute-start.1 = (f32[3,1,128,128]{3,2,1,0:T(8,128)S(1)}, f32[3,1,128,128]{3,2,1,0:T(8,128)S(1)}, u32[]{:S(2)}, u32[]{:S(2)}) collective-permute-start(f32[3,1,128,128]{3,2,1,0:T(8,128)S(1)} %get-tuple-element.36), channel_id=1, source_target_pairs={{0,1},{1,2},{2,3},{3,4},{4,5},{5,6},{6,7},{7,8},{8,9},{9,10},{10,1... | collective-permute-start | bytes 589832 | tf_op jit(solution)/shard_map/ppermute | solution.py:17
  7.0 7.4 %copy-start.1 = (f32[2,128,128]{2,1,0:T(8,128)S(1)}, f32[2,128,128]{2,1,0:T(8,128)}, u32[]{:S(2)}) copy-start(f32[2,128,128]{2,1,0:T(8,128)} %param.3) | copy-start | bytes 393220
  15.4 3.2 %collective-permute-start.2 = (f32[3,1,128,128]{3,2,1,0:T(8,128)S(1)}, f32[3,1,128,128]{3,2,1,0:T(8,128)S(1)}, u32[]{:S(2)}, u32[]{:S(2)}) collective-permute-start(f32[3,1,128,128]{3,2,1,0:T(8,128)S(1)} %get-tuple-element.22), channel_id=1, source_target_pairs={{1,0},{2,1},{3,2},{4,3},{5,4},{6,5},{7,6},{8,7},{9,8},{10,9},{11,1... | collective-permute-start | bytes 589832 | tf_op jit(solution)/shard_map/ppermute | solution.py:19
  15.5 7.8 %collective-permute-start.3 = (f32[3,1,128,128]{3,2,1,0:T(8,128)S(1)}, f32[3,1,128,128]{3,2,1,0:T(8,128)S(1)}, u32[]{:S(2)}, u32[]{:S(2)}) collective-permute-start(f32[3,1,128,128]{3,2,1,0:T(8,128)S(1)} %get-tuple-element.23), channel_id=1, source_target_pairs={{0,1},{1,2},{2,3},{3,4},{4,5},{5,6},{6,7},{7,8},{8,9},{9,10},{10,1... | collective-permute-start | bytes 589832 | tf_op jit(solution)/shard_map/ppermute | solution.py:17
  23.9 8.7 %collective-permute-start.4 = (f32[3,2,128,128]{3,2,1,0:T(8,128)S(1)}, f32[3,2,128,128]{3,2,1,0:T(8,128)S(1)}, u32[]{:S(2)}, u32[]{:S(2)}) collective-permute-start(f32[3,2,128,128]{3,2,1,0:T(8,128)S(1)} %get-tuple-element.5), channel_id=1, source_target_pairs={{0,16},{1,17},{2,18},{3,19},{4,20},{5,21},{6,22},{7,23},{8,24},{9,... | collective-permute-start | bytes 1179656 | tf_op jit(solution)/shard_map/ppermute | solution.py:29
  33.1 4.6 %collective-permute-start.5 = (f32[3,1,128,128]{3,2,1,0:T(8,128)S(1)}, f32[3,1,128,128]{3,2,1,0:T(8,128)S(1)}, u32[]{:S(2)}, u32[]{:S(2)}) collective-permute-start(f32[3,1,128,128]{3,2,1,0:T(8,128)S(1)} %get-tuple-element.13), channel_id=1, source_target_pairs={{1,0},{2,1},{3,2},{4,3},{5,4},{6,5},{7,6},{8,7},{9,8},{10,9},{11,1... | collective-permute-start | bytes 589832 | tf_op jit(solution)/shard_map/ppermute | solution.py:19
  34.5 7.8 %collective-permute-start.6 = (f32[3,1,128,128]{3,2,1,0:T(8,128)S(1)}, f32[3,1,128,128]{3,2,1,0:T(8,128)S(1)}, u32[]{:S(2)}, u32[]{:S(2)}) collective-permute-start(f32[3,1,128,128]{3,2,1,0:T(8,128)S(1)} %get-tuple-element.12), channel_id=1, source_target_pairs={{0,1},{1,2},{2,3},{3,4},{4,5},{5,6},{6,7},{7,8},{8,9},{9,10},{10,1... | collective-permute-start | bytes 589832 | tf_op jit(solution)/shard_map/ppermute | solution.py:17
where the time goes:
time: 43.6 us; the launch traced here: 43.5 us
  waiting for transfers between devices  27.7 us (64%)
  starting transfers between devices  10.8 us (25%)
  local copies, waits for them, and re-layouts  2.52 us (6%)
  other arithmetic  2.28 us (5%)
    ppermute x3, waiting for transfers between devices, padded_2(): lax.ppermute(tail, axis, [(i, (i + 1) % count) for i in range(count)])  13.9 us
    ppermute x3, waiting for transfers between devices, padded_2(): lax.ppermute(head, axis, [((i + 1) % count, i) for i in range(count)])  8.55 us
    ppermute x3, starting transfers between devices, padded_2(): lax.ppermute(head, axis, [((i + 1) % count, i) for i in range(count)])  6.92 us
    ppermute x1, waiting for transfers between devices, from_behind(): lax.ppermute(value, axis, [(source, source + steps) for source in range(f...  5.25 us
    ppermute x1, starting transfers between devices, from_behind(): lax.ppermute(value, axis, [(source, source + steps) for source in range(f...  3.42 us
    broadcast_in_dim x1, other arithmetic, local(): return start[None]  1.22 us
    slice x2, local copies, waits for them, and re-layouts, padded_2(): head = lax.slice_in_dim(cells, 0, width, axis=dim)  1.13 us
    slice x6, local copies, waits for them, and re-layouts, advance_with(): x_plus = jnp.roll(center, -1, axis=-1)  1.09 us
  transfers between devices with their start and end apart: 7, of which 7 were waited for; matrix products, arithmetic and copies ran while one was open for 1% of the time, Pallas kernels for 0%

commit v1 on v0

v1 whole, which is shorter than its diff:
```python
import functools

import jax
import jax.numpy as jnp
from jax import lax
from jax.experimental import pallas as pl
from jax.experimental.pallas import tpu as pltpu
from jax.sharding import PartitionSpec as P

FINE_STEP = 0.12
COARSE_STEP = 0.24
MESH = pl.DeviceIdType.MESH
TILE = 8


def row_plan(tiles):
    cuts = [0] + [max(1, tiles * part // 16) for part in (6, 10, 14)] + [tiles]
    chunks = [(a, b) for a, b in zip(cuts, cuts[1:]) if b > a]
    fine_one, fine_two = [], []
    done_one, done_two = 1, 2
    for _, end in chunks:
        last = end == tiles
        upto_one = tiles + 1 if last else max(done_one, end - 1)
        upto_two = tiles + 2 if last else max(done_two, end - 2)
        fine_one.append((done_one, upto_one))
        fine_two.append((done_two, upto_two))
        done_one, done_two = upto_one, upto_two
    return chunks, fine_one, fine_two


def pieces_of(first, last, tiles):
    pieces = []
    if first < min(last, tiles):
        pieces.append((first, min(last, tiles)))
    if last > tiles:
        pieces.append((max(first, tiles) - tiles, last - tiles))
    return pieces


def rates(ref, plane, row, visc, nx):
    center = [ref[c, plane, pl.ds(row, TILE), :] for c in range(3)]
    out = []
    for c in range(3):
        u = center[c]
        above = ref[c, plane + 1, pl.ds(row, TILE), :]
        below = ref[c, plane - 1, pl.ds(row, TILE), :]
        y_plus = ref[c, plane, pl.ds(row + 1, TILE), :]
        y_minus = ref[c, plane, pl.ds(row - 1, TILE), :]
        x_plus = pltpu.roll(u, nx - 1, 1)
        x_minus = pltpu.roll(u, 1, 1)
        laplace = (above + below) + (y_plus + y_minus) + (x_plus + x_minus) - 6.0 * u
        carried = (
            center[0] * (above - below)
            + center[1] * (y_plus - y_minus)
            + center[2] * (x_plus - x_minus)
        )
        out.append(visc * laplace - 0.5 * carried)
    return center, out


def kernel(
    count, groups, states, viscosity, result,
    field, visc, fine, jump, start,
    own_sem, send_s, recv_s, send_v, recv_v, send_c, recv_c, send_h, recv_h,
):
    _, _, nz, ny, nx = states.shape
    tiles = ny // TILE
    chunks, fine_one, fine_two = row_plan(tiles)
    pieces = [pieces_of(first, last, tiles) for first, last in fine_two]
    numbered, serial = [], 0
    for group in pieces:
        numbered.append([(serial + k, a, b) for k, (a, b) in enumerate(group)])
        serial += len(group)

    me = lax.axis_index("space")
    turn = lax.axis_index("tm")
    right = lax.rem(me + 1, count)
    left = lax.rem(me + count - 1, count)

    own_state = pltpu.make_async_copy(
        states.at[0], field.at[:, pl.ds(2, nz), pl.ds(TILE, ny), :], own_sem.at[0])
    own_visc = pltpu.make_async_copy(viscosity, visc.at[pl.ds(1, nz)], own_sem.at[1])
    own_state.start()
    own_visc.start()

    def next_turn():
        return {"tm": turn + 1}

    barrier = pltpu.get_barrier_semaphore()
    for side in (left, right):
        pl.semaphore_signal(barrier, inc=1, device_id={"space": side}, device_id_type=MESH)
    if groups > 1:
        @pl.when(turn > 0)
        def _():
            pl.semaphore_signal(barrier, inc=1, device_id={"tm": turn - 1}, device_id_type=MESH)

        @pl.when(turn < groups - 1)
        def _():
            pl.semaphore_signal(barrier, inc=1, device_id=next_turn(), device_id_type=MESH)

    peers = 2 + (turn > 0).astype(jnp.int32) + (turn < groups - 1).astype(jnp.int32)
    pl.semaphore_wait(barrier, peers)

    def halo_copies(k):
        first, last = chunks[k]
        rows = pl.ds(first * TILE, (last - first) * TILE)
        padded = pl.ds((first + 1) * TILE, (last - first) * TILE)
        copies = []
        for d, (side, src, dst, vsrc, vdst) in enumerate((
            (right, nz - 2, 0, nz - 1, 0),
            (left, 0, nz + 2, 0, nz + 1),
        )):
            copies.append(pltpu.make_async_remote_copy(
                viscosity.at[vsrc, rows, :], visc.at[vdst, rows, :],
                send_v.at[d, k], recv_v.at[d, k],
                device_id={"space": side}, device_id_type=MESH))
            copies.append(pltpu.make_async_remote_copy(
                states.at[0, :, pl.ds(src, 2), rows, :], field.at[:, pl.ds(dst, 2), padded, :],
                send_s.at[d, k], recv_s.at[d, k],
                device_id={"space": side}, device_id_type=MESH))
        return copies

    def pass_copy(i, a, b):
        rows = pl.ds(a * TILE, (b - a) * TILE)
        padded = pl.ds((a + 1) * TILE, (b - a) * TILE)
        return pltpu.make_async_remote_copy(
            result.at[0, :, :, rows, :], start.at[:, pl.ds(1, nz), padded, :],
            send_c.at[i], recv_c.at[i], device_id=next_turn(), device_id_type=MESH)

    def edge_copies(i, a, b):
        padded = pl.ds((a + 1) * TILE, (b - a) * TILE)
        return [
            pltpu.make_async_remote_copy(
                start.at[:, src, padded, :], start.at[:, dst, padded, :],
                send_h.at[d, i], recv_h.at[d, i],
                device_id={"space": side}, device_id_type=MESH)
            for d, (side, src, dst) in enumerate(((right, nz, 0), (left, 1, nz + 1)))
        ]

    halos = [halo_copies(k) for k in range(len(chunks))]
    for copies in halos:
        for copy in copies:
            copy.start()
    own_state.wait()
    own_visc.wait()

    def wrap_rows(ref):
        for c in range(3):
            for plane in range(ref.shape[1]):
                ref[c, plane, pl.ds(TILE - 1, 1), :] = ref[c, plane, pl.ds(TILE + ny - 1, 1), :]
                ref[c, plane, pl.ds(TILE + ny, 1), :] = ref[c, plane, pl.ds(TILE, 1), :]

    def first_step(t, _):
        row = lax.rem(t, tiles) * TILE
        for plane in range(nz + 2):
            here, rate = rates(field, plane + 1, row + TILE, visc[plane, pl.ds(row, TILE), :], nx)
            for c in range(3):
                fine[c, plane, pl.ds(row + TILE, TILE), :] = here[c] + FINE_STEP * rate[c]
                if 1 <= plane <= nz:
                    jump[c, plane - 1, pl.ds(row, TILE), :] = here[c] + COARSE_STEP * rate[c]
        return _

    def second_step(t, _):
        row = lax.rem(t, tiles) * TILE
        for plane in range(nz):
            here, rate = rates(
                fine, plane + 1, row + TILE, visc[plane + 1, pl.ds(row, TILE), :], nx)
            for c in range(3):
                coarse = jump[c, plane, pl.ds(row, TILE), :]
                change = here[c] + FINE_STEP * rate[c] - coarse
                jump[c, plane, pl.ds(row, TILE), :] = change
                result[0, c, plane, pl.ds(row, TILE), :] = coarse + change
        return _

    def correct(t, _):
        row = t * TILE
        for plane in range(nz):
            here, rate = rates(
                start, plane + 1, row + TILE, visc[plane + 1, pl.ds(row, TILE), :], nx)
            for c in range(3):
                result[0, c, plane, pl.ds(row, TILE), :] = (
                    here[c] + COARSE_STEP * rate[c] + jump[c, plane, pl.ds(row, TILE), :])
        return _

    def hand_on(group):
        if groups > 1 and group:
            @pl.when(turn == 0)
            def _():
                for piece in group:
                    pass_copy(*piece).start()

    def take_over(group):
        if groups > 1 and group:
            @pl.when(turn > 0)
            def _():
                for piece in group:
                    pass_copy(*piece).wait_recv()
                    for copy in edge_copies(*piece):
                        copy.start()

    for k in range(len(chunks)):
        for copy in halos[k]:
            copy.wait_recv()
        last = k == len(chunks) - 1
        if last:
            wrap_rows(field)
        lax.fori_loop(*fine_one[k], first_step, None)
        if last:
            wrap_rows(fine)
        lax.fori_loop(*fine_two[k], second_step, None)
        hand_on(numbered[k])
        if groups == 2 and k > 0:
            take_over(numbered[k - 1])

    if groups > 1:
        @pl.when(turn > 0)
        def _():
            for k in range(len(chunks)):
                if groups > 2 or k == len(chunks) - 1:
                    for piece in numbered[k]:
                        pass_copy(*piece).wait_recv()
                        for copy in edge_copies(*piece):
                            copy.start()
            for group in numbered:
                for piece in group:
                    for copy in edge_copies(*piece):
                        copy.wait_recv()
            wrap_rows(start)
            lax.fori_loop(0, tiles, correct, None)

            @pl.when(turn < groups - 1)
            def _():
                for group in numbered:
                    for piece in group:
                        pass_copy(*piece).start()

            for group in numbered:
                for piece in group:
                    for copy in edge_copies(*piece):
                        copy.wait_send()

        @pl.when(turn < groups - 1)
        def _():
            for group in numbered:
                for piece in group:
                    pass_copy(*piece).wait_send()

    for copies in halos:
        for copy in copies:
            copy.wait_send()


def local(count, groups, states, viscosity):
    _, _, nz, ny, nx = states.shape
    chunks, _, fine_two = row_plan(ny // TILE)
    passes = sum(len(pieces_of(a, b, ny // TILE)) for a, b in fine_two)
    padded = ny + 2 * TILE
    f32 = jnp.float32
    dma = pltpu.SemaphoreType.DMA
    return pl.pallas_call(
        functools.partial(kernel, count, groups),
        out_shape=jax.ShapeDtypeStruct(states.shape, f32),
        in_specs=[pl.BlockSpec(memory_space=pl.ANY)] * 2,
        out_specs=pl.BlockSpec(memory_space=pltpu.VMEM),
        scratch_shapes=[
            pltpu.VMEM((3, nz + 4, padded, nx), f32),
            pltpu.VMEM((nz + 2, ny, nx), f32),
            pltpu.VMEM((3, nz + 2, padded, nx), f32),
            pltpu.VMEM((3, nz, ny, nx), f32),
            pltpu.VMEM((3, nz + 2, padded, nx), f32),
            dma((2,)),
            dma((2, len(chunks))),
            dma((2, len(chunks))),
            dma((2, len(chunks))),
            dma((2, len(chunks))),
            dma((passes,)),
            dma((passes,)),
            dma((2, passes)),
            dma((2, passes)),
        ],
        compiler_params=pltpu.CompilerParams(
            collective_id=0, has_side_effects=True, vmem_limit_bytes=32 * 1024 * 1024),
    )(states, viscosity)


def solution(mesh):
    return jax.shard_map(
        functools.partial(local, mesh.shape["space"], mesh.shape["tm"]),
        mesh=mesh,
        in_specs=(P("tm", None, "space", None, None), P("space", None, None)),
        out_specs=P("tm", None, "space", None, None),
        check_vma=False,
    )
```

time: 43.6 us -> 26.8 us (0.61)
  the two profiles are of different devices: /device:TPU:0 before, /device:TPU:6 now
where the time goes in v1:
time: 26.8 us; the launch traced here: 26.7 us
  Pallas kernels  24 us (90%)
  local copies, waits for them, and re-layouts  2.65 us (10%)
    pallas_call x1, Pallas kernels, local(): pl.pallas_call(functools.partial(kernel, count, groups), out_shape=jax.Sh...  24 us
    unnamed x5, local copies, waits for them, and re-layouts  2.65 us

profile of v1, /device:TPU:6, one launch (start us, length us, event | category | flops | bytes accessed | tf_op | source)
XLA Modules:
  0.0 26.7 jit_solution(1549095345572342104)
XLA Ops:
  0.0 0.0 copy-start
  0.0 1.0 %copy-done = f32[1,3,2,128,128]{4,3,2,1,0:T(8,128)S(1)} copy-done((f32[1,3,2,128,128]{4,3,2,1,0:T(8,128)S(1)}, f32[1,3,2,128,128]{4,3,2,1,0:T(8,128)}, u32[]{:S(2)}) %copy-start) | copy-done | bytes 393240
  1.0 0.0 copy-start.1
  1.0 0.9 %copy-done.1 = f32[2,128,128]{2,1,0:T(8,128)S(1)} copy-done((f32[2,128,128]{2,1,0:T(8,128)S(1)}, f32[2,128,128]{2,1,0:T(8,128)}, u32[]{:S(2)}) %copy-start.1) | copy-done | bytes 131096
  1.9 24.0 %shard_map.28 = f32[1,3,2,128,128]{4,3,2,1,0:T(8,128)S(1)} custom-call(f32[1,3,2,128,128]{4,3,2,1,0:T(8,128)S(1)} %copy-done, f32[2,128,128]{2,1,0:T(8,128)S(1)} %copy-done.1), custom_call_target="tpu_custom_call" | custom-call | tf_op jit(solution)/shard_map/pallas_call | solution.py:260
  25.9 0.7 %copy.4 = f32[1,3,2,128,128]{4,3,2,1,0:T(8,128)} copy(f32[1,3,2,128,128]{4,3,2,1,0:T(8,128)S(1)} %shard_map.28) | data formatting | bytes 786432
Async XLA Ops:
  0.0 1.0 %copy-start = (f32[1,3,2,128,128]{4,3,2,1,0:T(8,128)S(1)}, f32[1,3,2,128,128]{4,3,2,1,0:T(8,128)}, u32[]{:S(2)}) copy-start(f32[1,3,2,128,128]{4,3,2,1,0:T(8,128)} %states.1) | copy-start | bytes 1179652
  1.0 0.9 %copy-start.1 = (f32[2,128,128]{2,1,0:T(8,128)S(1)}, f32[2,128,128]{2,1,0:T(8,128)}, u32[]{:S(2)}) copy-start(f32[2,128,128]{2,1,0:T(8,128)} %viscosity.1) | copy-start | bytes 393220

commit v2 on v1

--- a/solution.py
+++ b/solution.py
@@ -11,6 +11,8 @@
 COARSE_STEP = 0.24
 MESH = pl.DeviceIdType.MESH
 TILE = 8
+MOST = 4
+UNROLL = 2
 
 
 def row_plan(tiles):
@@ -30,10 +32,11 @@
 
 def pieces_of(first, last, tiles):
     pieces = []
-    if first < min(last, tiles):
-        pieces.append((first, min(last, tiles)))
-    if last > tiles:
-        pieces.append((max(first, tiles) - tiles, last - tiles))
+    while first < last:
+        begin = first % tiles
+        length = min(MOST, last - first, tiles - begin)
+        pieces.append((begin, begin + length))
+        first += length
     return pieces
 
 
@@ -173,7 +176,7 @@
         return _
 
     def correct(t, _):
-        row = t * TILE
+        row = lax.rem(t, tiles) * TILE
         for plane in range(nz):
             here, rate = rates(
                 start, plane + 1, row + TILE, visc[plane + 1, pl.ds(row, TILE), :], nx)
@@ -204,11 +207,12 @@
         last = k == len(chunks) - 1
         if last:
             wrap_rows(field)
-        lax.fori_loop(*fine_one[k], first_step, None)
+        lax.fori_loop(*fine_one[k], first_step, None, unroll=UNROLL)
         if last:
             wrap_rows(fine)
-        lax.fori_loop(*fine_two[k], second_step, None)
-        hand_on(numbered[k])
+        for piece in numbered[k]:
+            lax.fori_loop(piece[1], piece[2], second_step, None, unroll=UNROLL)
+            hand_on([piece])
         if groups == 2 and k > 0:
             take_over(numbered[k - 1])
 
@@ -221,12 +225,17 @@
                         pass_copy(*piece).wait_recv()
                         for copy in edge_copies(*piece):
                             copy.start()
-            for group in numbered:
+            done = 3
+            for (_, upto), group in zip(fine_two, numbered):
                 for piece in group:
                     for copy in edge_copies(*piece):
                         copy.wait_recv()
-            wrap_rows(start)
-            lax.fori_loop(0, tiles, correct, None)
+                upto = upto + 1 if upto > tiles else upto - 1
+                if upto > tiles:
+                    wrap_rows(start)
+                if upto > done:
+                    lax.fori_loop(done, upto, correct, None, unroll=UNROLL)
+                    done = upto
 
             @pl.when(turn < groups - 1)
             def _():
@@ -259,7 +268,7 @@
     dma = pltpu.SemaphoreType.DMA
     return pl.pallas_call(
         functools.partial(kernel, count, groups),
-        out_shape=jax.ShapeDtypeStruct(states.shape, f32),
+        out_shape=pltpu.VMEM(states.shape, f32),
         in_specs=[pl.BlockSpec(memory_space=pl.ANY)] * 2,
         out_specs=pl.BlockSpec(memory_space=pltpu.VMEM),
         scratch_shapes=[
@@ -279,8 +288,11 @@
             dma((2, passes)),
         ],
         compiler_params=pltpu.CompilerParams(
-            collective_id=0, has_side_effects=True, vmem_limit_bytes=32 * 1024 * 1024),
-    )(states, viscosity)
+            collective_id=0, has_side_effects=True),
+    )(
+        pltpu.with_memory_space_constraint(states, pltpu.HBM),
+        pltpu.with_memory_space_constraint(viscosity, pltpu.HBM),
+    )
 
 
 def solution(mesh):

time: 26.8 us -> 23.6 us (0.88)
  local copies, waits for them, and re-layouts: 2.65 us -> 0.75 us
  Pallas kernels: 24 us -> 22.7 us
    unnamed x5 -> x1, local copies, waits for them, and re-layouts: 2.65 us -> 0.75 us
    pallas_call x1, Pallas kernels: 24 us -> 22.7 us  [local(): pl.pallas_call(functools.partial(kernel, count, groups), out_shape=pltpu....]
where the time goes in v2:
time: 23.6 us; the launch traced here: 23.5 us
  Pallas kernels  22.7 us (96%)
  local copies, waits for them, and re-layouts  0.75 us (3%)
    pallas_call x1, Pallas kernels, local(): pl.pallas_call(functools.partial(kernel, count, groups), out_shape=pltpu....  22.7 us
    unnamed x1, local copies, waits for them, and re-layouts  0.75 us

profile of v2, /device:TPU:6, one launch (start us, length us, event | category | flops | bytes accessed | tf_op | source)
XLA Modules:
  0.0 23.5 jit_solution(12793184330415918015)
XLA Ops:
  0.0 22.7 %shard_map.28 = f32[1,3,2,128,128]{4,3,2,1,0:T(8,128)S(1)} custom-call(f32[1,3,2,128,128]{4,3,2,1,0:T(8,128)} %states.1, f32[2,128,128]{2,1,0:T(8,128)} %viscosity.1), custom_call_target="tpu_custom_call" | custom-call | tf_op jit(solution)/shard_map/pallas_call | solution.py:269
  22.7 0.7 %copy.4 = f32[1,3,2,128,128]{4,3,2,1,0:T(8,128)} copy(f32[1,3,2,128,128]{4,3,2,1,0:T(8,128)S(1)} %shard_map.28) | data formatting | bytes 786432

commit v3 on v2

--- a/solution.py
+++ b/solution.py
@@ -16,7 +16,7 @@
 
 
 def row_plan(tiles):
-    cuts = [0] + [max(1, tiles * part // 16) for part in (6, 10, 14)] + [tiles]
+    cuts = [0] + [max(1, tiles * part // 16) for part in (5, 8, 11, 14)] + [tiles]
     chunks = [(a, b) for a, b in zip(cuts, cuts[1:]) if b > a]
     fine_one, fine_two = [], []
     done_one, done_two = 1, 2
@@ -79,6 +79,7 @@
     turn = lax.axis_index("tm")
     right = lax.rem(me + 1, count)
     left = lax.rem(me + count - 1, count)
+    odd = lax.rem(me, 2)
 
     own_state = pltpu.make_async_copy(
         states.at[0], field.at[:, pl.ds(2, nz), pl.ds(TILE, ny), :], own_sem.at[0])
@@ -109,10 +110,10 @@
         rows = pl.ds(first * TILE, (last - first) * TILE)
         padded = pl.ds((first + 1) * TILE, (last - first) * TILE)
         copies = []
-        for d, (side, src, dst, vsrc, vdst) in enumerate((
-            (right, nz - 2, 0, nz - 1, 0),
-            (left, 0, nz + 2, 0, nz + 1),
-        )):
+        for d in (1 - odd, odd):
+            side = lax.rem(me + 1 + d * (count - 2), count)
+            src, dst = (1 - d) * (nz - 2), d * (nz + 2)
+            vsrc, vdst = (1 - d) * (nz - 1), d * (nz + 1)
             copies.append(pltpu.make_async_remote_copy(
                 viscosity.at[vsrc, rows, :], visc.at[vdst, rows, :],
                 send_v.at[d, k], recv_v.at[d, k],

time: 23.6 us -> 23.4 us (level)
  no operation moved by 1% of the time
where the time goes in v3:
time: 23.4 us; the launch traced here: 23.3 us
  Pallas kernels  22.6 us (97%)
  local copies, waits for them, and re-layouts  0.75 us (3%)
    pallas_call x1, Pallas kernels, local(): pl.pallas_call(functools.partial(kernel, count, groups), out_shape=pltpu....  22.6 us
    unnamed x1, local copies, waits for them, and re-layouts  0.75 us

profile of v3, /device:TPU:6, one launch (start us, length us, event | category | flops | bytes accessed | tf_op | source)
XLA Modules:
  0.0 23.3 jit_solution(17748873425189191116)
XLA Ops:
  0.0 22.6 %shard_map.28 = f32[1,3,2,128,128]{4,3,2,1,0:T(8,128)S(1)} custom-call(f32[1,3,2,128,128]{4,3,2,1,0:T(8,128)} %states.1, f32[2,128,128]{2,1,0:T(8,128)} %viscosity.1), custom_call_target="tpu_custom_call" | custom-call | tf_op jit(solution)/shard_map/pallas_call | solution.py:270
  22.6 0.7 %copy.4 = f32[1,3,2,128,128]{4,3,2,1,0:T(8,128)} copy(f32[1,3,2,128,128]{4,3,2,1,0:T(8,128)S(1)} %shard_map.28) | data formatting | bytes 786432
